TPU v7x, 32 devices: a whole 2x2x4 slice. The times are simulated.
32 devices in a mesh: ka: 16 (over z, y, x), br: 2 (over core).
Axes of the slice: x: 2, y: 2, z: 4, core: 2. Of those that a mesh axis runs over, the one named last changes fastest.
Arguments:
- occupation: float32 [8, 8192], P(None, 'ka'), may hold values from 0 to 1
- phonons: float32 [12, 4096], P('br', 'ka'), may hold values from 0.05 to 5
- coupling: bfloat16 [16, 12, 8, 8, 8192], P(None, 'br', None, None, 'ka'), may hold values from 0.00049972534 to 0.0079956055
- shifted_point_index: int32 [16, 8192], P(None, 'ka'), may hold values from 0 to 8191
- wavevector_index: int32 [16, 8192], P(None, 'ka'), may hold values from 0 to 4095
- window: int32 [8, 8192], P(None, 'ka'), may hold values 0 or 1
Outputs:
- collision: float32 [8, 8192], P(None, 'ka')
- generation: float32 [12, 4096], P('br', 'ka')
All inputs are finite; a program needn't handle non-finite values. No bound on the sum of `window` on one device may be relied on, other than what follows from the above.
Results may differ from a plain program's by a relative error of at most 0.0003.
Values sent between devices are 32-bit elements; how exact they have to be, the bound alone decides.
A program may use at most 128 MiB of HBM per device.

v0:
```python
import jax
import jax.numpy as jnp
from jax import lax
from jax.sharding import PartitionSpec as P


def fetch_states(occupation, phonon_share, shifted_point_index):
    collected_values, phonon_full = (
        lax.all_gather(occupation, "ka", axis=1, tiled=True),
        lax.all_gather(phonon_share, "ka", axis=1, tiled=True),
    )
    picked = jnp.take(collected_values, shifted_point_index, axis=1)
    return (jnp.transpose(picked, (1, 0, 2)), phonon_full)


def share_generation(term):
    return lax.psum_scatter(term, "ka", scatter_dimension=1, tiled=True)


def apply_scattering(occupation, beyond_all, phonon_full, coupling, wavevector_index, window):
    window_f = window.astype(jnp.float32)
    num_q = phonon_full.shape[1]

    def slot_step(loop_state, inputs):
        scattering_sum, emission_sum = loop_state
        tile, beyond, q_rows = inputs
        tile = tile.astype(jnp.float32)
        phonon_at = phonon_full[:, q_rows]
        weighted = jnp.einsum("umnk,nk->umk", tile, beyond)
        totals = jnp.sum(tile, axis=2)
        detailed_balance_term = window_f[None] * (
            weighted * (phonon_at[:, None, :] + 1.0)
            - occupation[None] * weighted
            - occupation[None] * totals * phonon_at[:, None, :]
        )
        per_point = jnp.sum(detailed_balance_term, axis=1)
        collected_values = jax.ops.segment_sum(per_point.T, q_rows, num_segments=num_q).T
        return (
            (
                scattering_sum + jnp.sum(detailed_balance_term, axis=0),
                emission_sum + collected_values,
            ),
            None,
        )

    start = (jnp.zeros(occupation.shape, jnp.float32), jnp.zeros(phonon_full.shape, jnp.float32))
    result, _ = lax.scan(slot_step, start, (coupling, beyond_all, wavevector_index))
    collision = lax.psum(result[0], "br")
    return (collision, result[1] / 16.0)


def on_device(occupation, phonons, coupling, shifted_point_index, wavevector_index, window):
    beyond_first, phonon_full = fetch_states(occupation, phonons, shifted_point_index)
    initial_scattering, leading_term = apply_scattering(
        occupation, beyond_first, phonon_full, coupling, wavevector_index, window
    )
    initial_emission = share_generation(leading_term)
    mid_phonons = phonons + 0.1 * initial_emission
    halfway_occupancy = occupation + 0.1 * initial_scattering
    beyond_second, mid_full = fetch_states(halfway_occupancy, mid_phonons, shifted_point_index)
    collision, second_term = apply_scattering(
        halfway_occupancy, beyond_second, mid_full, coupling, wavevector_index, window
    )
    generation = share_generation(second_term)
    return (collision, generation)


def solution(mesh):
    in_specs = (
        P(None, "ka"),
        P("br", "ka"),
        P(None, "br", None, None, "ka"),
        P(None, "ka"),
        P(None, "ka"),
        P(None, "ka"),
    )
    out_specs = (P(None, "ka"), P("br", "ka"))
    return jax.shard_map(
        on_device, mesh=mesh, in_specs=in_specs, out_specs=out_specs, check_vma=False
    )
```

profile of v0, /device:TPU:0, one launch (start us, length us, event | category | flops | bytes accessed | tf_op | source)
XLA Modules:
  0.0 856.6 jit_solution(11544250509891462724)
XLA Ops:
  9.6 98.0 %all_gather.12 = f32[8,8192]{0,1:T(8,128)} all-gather(f32[8,512]{0,1:T(8,128)S(1)} %copy.60), channel_id=1, replica_groups=mesh['ka'=16,'br'=2] {'ka'}, dimensions={1}, use_global_device_ids=true | all-gather | bytes 278528 | tf_op jit(solution)/shard_map/all_gather | solution.py:9
  107.6 29.9 %gather_fusion.2 = f32[8192,8]{1,0:T(8,128)} fusion(f32[8,8192]{0,1:T(8,128)} %all_gather.12, s32[8192]{0:T(1024)S(1)} %broadcast_clamp_fusion), kind=kCustom, calls=%fused_computation.clone | custom fusion | bytes 557056 | tf_op jit(solution)/shard_map/jit(_take)/gather | solution.py:12
  140.5 67.9 %all_gather.13 = f32[6,4096]{0,1:T(8,128)} all-gather(f32[6,256]{0,1:T(8,128)S(1)} %copy.58), channel_id=1, replica_groups=mesh['ka'=16,'br'=2] {'ka'}, dimensions={1}, use_global_device_ids=true | all-gather | bytes 104448 | tf_op jit(solution)/shard_map/all_gather | solution.py:10
  208.5 193.9 %while.26 = (s32[]{:T(128)}, f32[8,512]{1,0:T(8,128)S(1)}, f32[6,4096]{0,1:T(8,128)}, f32[8,512]{1,0:T(8,128)S(1)}, f32[16,8,512]{2,1,0:T(8,128)S(1)}, /*index=5...) while((s32[]{:T(128)}, f32[8,512]{1,0:T(8,128)S(1)}, ...), condition=%wide.region_5.7_spmd.clone, body=%wide.region_0.6_spmd.clone.sunk | while | flops 1213955 | bytes 1869972 | solution.py:47
  228.1 3.2 bitcast_add_fusion.4
  240.4 3.2 bitcast_add_fusion.4
  252.6 3.2 bitcast_add_fusion.4
  264.8 3.2 bitcast_add_fusion.4
  277.0 3.2 bitcast_add_fusion.4
  289.2 3.2 bitcast_add_fusion.4
  301.4 3.2 bitcast_add_fusion.4
  313.7 3.2 bitcast_add_fusion.4
  325.9 3.2 bitcast_add_fusion.4
  338.1 3.2 bitcast_add_fusion.4
  350.3 3.2 bitcast_add_fusion.4
  362.5 3.2 bitcast_add_fusion.4
  374.7 3.2 bitcast_add_fusion.4
  387.0 3.2 bitcast_add_fusion.4
  399.2 3.2 bitcast_add_fusion.4
  405.5 4.0 psum.14
  409.5 97.2 %all_gather.14 = f32[8,8192]{0,1:T(8,128)} all-gather(f32[8,512]{0,1:T(8,128)S(1)} %multiply_add_fusion), channel_id=1, replica_groups=mesh['ka'=16,'br'=2] {'ka'}, dimensions={1}, use_global_device_ids=true | all-gather | bytes 278528 | tf_op jit(solution)/shard_map/all_gather | solution.py:9
  506.8 29.9 %gather_fusion.3 = f32[8192,8]{1,0:T(8,128)} fusion(f32[8,8192]{0,1:T(8,128)} %all_gather.14, s32[8192]{0:T(1024)S(1)} %broadcast_clamp_fusion), kind=kCustom, calls=%fused_computation.3.clone | custom fusion | bytes 557056 | tf_op jit(solution)/shard_map/jit(_take)/gather | solution.py:12
  540.3 38.6 %all_gather.15 = f32[6,4096]{1,0:T(8,128)S(1)} all-gather(f32[6,256]{1,0:T(8,128)S(1)} %multiply_add_fusion.1), channel_id=1, replica_groups=mesh['ka'=16,'br'=2] {'ka'}, dimensions={1}, use_global_device_ids=true | all-gather | bytes 104448 | tf_op jit(solution)/shard_map/all_gather | solution.py:10
  580.9 193.9 %while.27 = (s32[]{:T(128)}, f32[8,512]{1,0:T(8,128)S(1)}, f32[6,4096]{0,1:T(8,128)}, f32[8,512]{1,0:T(8,128)S(1)}, f32[16,8,512]{2,1,0:T(8,128)S(1)}, /*index=5...) while((s32[]{:T(128)}, f32[8,512]{1,0:T(8,128)S(1)}, ...), condition=%wide.region_13.15_spmd.clone, body=%wide.region_8.0_spmd.clone.sunk | while | flops 1213955 | bytes 1869972 | solution.py:47
  600.6 3.2 bitcast_add_fusion.5
  612.8 3.2 bitcast_add_fusion.5
  625.0 3.2 bitcast_add_fusion.5
  637.2 3.2 bitcast_add_fusion.5
  649.4 3.2 bitcast_add_fusion.5
  735.0 3.2 bitcast_add_fusion.5
  777.7 4.0 psum.15
  781.7 68.1 %reduce-scatter.5.cloned.1.call-done = f32[6,256]{1,0:T(8,128)} async-done(((f32[6,4096]{1,0:T(8,128)}), f32[6,256]{1,0:T(8,128)}) %reduce-scatter.5.cloned.1.call-update) | async-done | bytes 6160 | tf_op jit(solution)/shard_map/reduce_scatter | solution.py:17
  (430 shorter events, 336.1 us)
Async XLA Ops:
  7.2 532.5 %reduce-scatter.3.cloned.1.call-start = ((), (), s32[]{:S(2)}) async-start(), calls=%async_computation.2 | async-start | bytes 139264 | tf_op jit(solution)/shard_map/reduce_scatter | solution.py:17
  137.5 2.8 copy-start.2
  137.5 2.8 copy-start.1
  140.3 68.1 %copy-start = (f32[8,512]{1,0:T(8,128)S(1)}, f32[8,512]{1,0:T(8,128)}, u32[]{:S(2)}) copy-start(f32[8,512]{1,0:T(8,128)} %param.12) | copy-start | bytes 49156
  405.3 444.5 %reduce-scatter.5.cloned.1.call-start = ((), (), s32[]{:S(2)}) async-start(), calls=%async_computation.3 | async-start | bytes 139264 | tf_op jit(solution)/shard_map/reduce_scatter | solution.py:17
Sparse Core Ops, SparseCore 0:
  405.4 72.9 reduce-scatter.2
  777.8 71.8 reduce-scatter.4
where the time goes:
time: 863 us; the launch traced here: 857 us
  blocking collectives  310 us (36%)
  other arithmetic  298 us (35%)
  local copies, waits for them, and re-layouts  165 us (19%)
  waiting for transfers between devices  68.1 us (8%)
  between operations  14.2 us (2%)
    all_gather x2, blocking collectives, fetch_states(): lax.all_gather(occupation, 'ka', axis=1, tiled=True)  195 us
    all_gather x2, blocking collectives, fetch_states(): lax.all_gather(phonon_share, 'ka', axis=1, tiled=True)  107 us
    add x32, other arithmetic, slot_step(): emission_sum + collected_values  99.3 us
    scatter-add x32, other arithmetic, slot_step(): jax.ops.segment_sum(per_point.T, q_rows, num_segments=num_q)  88.3 us
    gather x64, local copies, waits for them, and re-layouts, slot_step(): phonon_at = phonon_full[:, q_rows]  87.3 us
    reduce_scatter x2, waiting for transfers between devices, share_generation(): return lax.psum_scatter(term, 'ka', scatter_dimension=1, tiled=True)  68.1 us
    gather x4, local copies, waits for them, and re-layouts, fetch_states(): picked = jnp.take(collected_values, shifted_point_index, axis=1)  65.4 us
    reduce_sum x32, other arithmetic, slot_step(): totals = jnp.sum(tile, axis=2)  40.7 us
  transfers between devices with their start and end apart: 2, of which 1 were waited for; matrix products, arithmetic and copies ran while one was open for 4% of the time, Pallas kernels for 0%

commit v1 on v0

v1 whole, which is shorter than its diff:
```python
import functools

import jax
import jax.numpy as jnp
from jax import lax
from jax.experimental import pallas as pl
from jax.experimental.pallas import tpu as pltpu
from jax.sharding import PartitionSpec as P

MESH = pl.DeviceIdType.MESH
F32 = jnp.float32
BF16 = jnp.bfloat16
LANES = 128


def quotient(x, size):
    if size & (size - 1) == 0:
        return lax.shift_right_logical(x, jnp.int32(size.bit_length() - 1))
    return lax.div(x, jnp.int32(size))


def remainder(x, size):
    if size & (size - 1) == 0:
        return lax.bitwise_and(x, jnp.int32(size - 1))
    return lax.rem(x, jnp.int32(size))


def split_terms(x):
    high = x.astype(BF16).astype(F32)
    return high, x - high


def step_kernel(
    n, nbr, branches,
    occ_ref, pho_ref, coup_hbm, kidx_ref, qidx_ref, win_ref,
    col_ref, gen_ref,
    coup, onehot_k, onehot_q, f_all, p_all, g_send, g_recv, c_send, c_recv,
    f_terms, p_terms, c_acc, g_acc, wf, ww,
    load_sem, fs_sem, fr_sem, ws_sem, wr_sem, ps_sem, pr_sem, gs_sem, gr_sem, cs_sem, cr_sem,
):
    me = lax.axis_index("ka")
    core = lax.axis_index("br")
    slots, bands, width = coup.shape[0], occ_ref.shape[0], occ_ref.shape[1]
    piece = width // nbr
    q_width = pho_ref.shape[1]
    rows = 8

    def load(s):
        return pltpu.make_async_copy(coup_hbm.at[s], coup.at[s], load_sem.at[s])

    def start_load(s, c):
        load(s).start()
        return c

    lax.fori_loop(0, slots, start_load, 0)

    def ahead(j):
        return lax.rem(me + j, n)

    def behind(j):
        return lax.rem(me - j + n, n)

    sibling = {"br": 1 - core}

    barrier = pltpu.get_barrier_semaphore()

    def greet(j, c):
        pl.semaphore_signal(barrier, inc=1, device_id={"ka": ahead(j)}, device_id_type=MESH)
        return c

    lax.fori_loop(1, n, greet, 0)
    pl.semaphore_signal(barrier, inc=1, device_id=sibling, device_id_type=MESH)
    pl.semaphore_wait(barrier, n)

    def f_copy(i, j):
        block = f_all.at[i, me, core]
        return pltpu.make_async_remote_copy(
            block, block, fs_sem.at[i, j], fr_sem.at[i, j], device_id={"ka": ahead(j)}, device_id_type=MESH)

    def f_forward(i, j):
        block = f_all.at[i, behind(j), core]
        return pltpu.make_async_remote_copy(
            block, block, ws_sem.at[i, j], wr_sem.at[i, j], device_id=sibling, device_id_type=MESH)

    def p_copy(i, j):
        block = p_all.at[i, me]
        return pltpu.make_async_remote_copy(
            block, block, ps_sem.at[i, j], pr_sem.at[i, j], device_id={"ka": ahead(j)}, device_id_type=MESH)

    def g_copy(i, j):
        return pltpu.make_async_remote_copy(
            g_send.at[i, ahead(j)], g_recv.at[i, me], gs_sem.at[i, j], gr_sem.at[i, j],
            device_id={"ka": ahead(j)}, device_id_type=MESH)

    def c_copy(i):
        return pltpu.make_async_remote_copy(
            c_send.at[i], c_recv.at[i], cs_sem.at[i], cr_sem.at[i], device_id=sibling, device_id_type=MESH)

    def each(do):
        def body(j, c):
            do(j)
            return c
        lax.fori_loop(1, n, body, 0)

    def send_f(i, f):
        for h in range(nbr):
            f_all[i, me, h] = f[:, h * piece:(h + 1) * piece]
        each(lambda j: f_copy(i, j).start())

    def send_p(i, p):
        p_all[i, me] = p
        each(lambda j: p_copy(i, j).start())

    def pass_on_f(i):
        def forward(j):
            f_copy(i, j).wait_recv()
            f_forward(i, j).start()
        each(forward)

    def collect_f(i):
        each(lambda j: f_forward(i, j).wait_recv())

        def body(a, c):
            both = jnp.concatenate([f_all[i, a, h] for h in range(nbr)], axis=0)
            high, low = split_terms(both)
            at = pl.ds(pl.multiple_of(a * nbr * rows, nbr * rows), nbr * rows)
            f_terms[0, at] = high.astype(BF16)
            f_terms[1, at] = low.astype(BF16)
            return c
        lax.fori_loop(0, n, body, 0)

    def collect_p(i):
        each(lambda j: p_copy(i, j).wait_recv())

        def body(a, c):
            both = jnp.concatenate([p_all[i, 2 * a], p_all[i, 2 * a + 1]], axis=0)
            high, low = split_terms(both)
            at = pl.ds(pl.multiple_of(a * 2 * rows, 2 * rows), 2 * rows)
            p_terms[0, at] = high.astype(BF16)
            p_terms[1, at] = low.astype(BF16)
            return c
        lax.fori_loop(0, n // 2, body, 0)

    def scatter_pass(i, f, window):
        for m in range(bands):
            ww[m] = jnp.broadcast_to(window[m:m + 1], (rows, width))
            wf[m] = jnp.broadcast_to((window * f)[m:m + 1], (rows, width))
        c_acc[...] = jnp.zeros_like(c_acc)
        g_acc[...] = jnp.zeros_like(g_acc)

        def body(s, carry):
            if i == 0:
                load(s).wait()
            k_high = quotient(kidx_ref[pl.ds(s, 1), :], piece)
            q_index = qidx_ref[pl.ds(s, 1), :]
            q_high = quotient(q_index, q_width)
            chunk = 2 * LANES
            for k0 in range(0, width, chunk):
                at = slice(k0, k0 + chunk)
                lk = onehot_k[s, :, at]
                lq = onehot_q[s, :, at]
                picked = jnp.dot(f_terms[0], lk, preferred_element_type=F32) + jnp.dot(
                    f_terms[1], lk, preferred_element_type=F32)
                kh = jnp.broadcast_to(k_high[:, at], (rows, chunk))
                e = jnp.zeros((rows, chunk), F32)
                for h in range(n * nbr):
                    e = jnp.where(kh == h, picked[h * rows:(h + 1) * rows], e)
                picked = jnp.dot(p_terms[0], lq, preferred_element_type=F32) + jnp.dot(
                    p_terms[1], lq, preferred_element_type=F32)
                qh = jnp.broadcast_to(q_high[:, at], (rows, chunk))
                w = jnp.zeros((rows, chunk), F32)
                for h in range(n):
                    w = jnp.where(qh == h, picked[h * rows:(h + 1) * rows], w)

                sums = []
                for k1 in range(0, chunk, LANES):
                    here = slice(k0 + k1, k0 + k1 + LANES)
                    e1 = e[:, k1:k1 + LANES]
                    w1 = w[:, k1:k1 + LANES]
                    row = lax.broadcasted_iota(jnp.int32, (rows, LANES), 0)
                    acc = [c_acc[m, :, here] for m in range(bands)]
                    t = jnp.zeros((rows, LANES), F32)
                    for u in range(branches):
                        wu = jnp.broadcast_to(w1[u:u + 1], (rows, LANES))
                        x = e1 * (wu + 1.0)
                        y = e1 + wu
                        total = None
                        for m in range(0, bands, 2):
                            first = (u * bands + m) * rows
                            g2 = coup[s, first:first + 2 * rows, here].astype(F32)
                            for d in range(2):
                                term = g2[d * rows:(d + 1) * rows] * (
                                    ww[m + d, :, here] * x - wf[m + d, :, here] * y)
                                acc[m + d] = acc[m + d] + term
                                total = term if total is None else total + term
                        t = jnp.where(row == u, jnp.sum(total, axis=0, keepdims=True), t)
                    for m in range(bands):
                        c_acc[m, :, here] = acc[m]
                    sums.append(t)
                t = jnp.concatenate(sums, axis=1)
                parts = [
                    jnp.where(qh == h, part, 0.0) for part in split_terms(t) for h in range(n)]
                spread = jnp.concatenate(parts, axis=0).astype(BF16)
                g_acc[...] += lax.dot_general(
                    spread, lq, (((1,), (1,)), ((), ())), preferred_element_type=F32)
            return carry

        lax.fori_loop(0, slots, body, 0)

        total = (g_acc[:n * rows] + g_acc[n * rows:]) * (1.0 / 16.0)
        g_send[i] = total.reshape(n, rows, q_width)
        each(lambda j: g_copy(i, j).start())
        mine = jnp.concatenate(
            [jnp.sum(c_acc[m], axis=0, keepdims=True) for m in range(bands)], axis=0)
        c_send[i] = mine
        c_copy(i).start()
        c_copy(i).wait_recv()
        return mine + c_recv[i]

    def finish_g(i):
        each(lambda j: g_copy(i, j).wait_recv())
        g_recv[i, me] = g_send[i, me]
        return jnp.sum(g_recv[i], axis=0)

    f0 = occ_ref[...]
    window = win_ref[...].astype(F32)
    send_f(0, f0)
    p0 = jnp.concatenate([pho_ref[...], jnp.zeros((rows - branches, q_width), F32)], axis=0)
    send_p(0, p0)

    def build(s, c):
        low_k = remainder(kidx_ref[pl.ds(s, 1), :], piece)
        low_q = remainder(qidx_ref[pl.ds(s, 1), :], q_width)
        onehot_k[s] = jnp.where(
            lax.broadcasted_iota(jnp.int32, (piece, width), 0) == low_k, 1.0, 0.0).astype(BF16)
        onehot_q[s] = jnp.where(
            lax.broadcasted_iota(jnp.int32, (q_width, width), 0) == low_q, 1.0, 0.0).astype(BF16)
        return c

    pass_on_f(0)
    lax.fori_loop(0, slots, build, 0)
    collect_f(0)
    collect_p(0)
    c0 = scatter_pass(0, f0, window)
    f1 = f0 + 0.1 * c0
    send_f(1, f1)
    p1 = p0 + 0.1 * finish_g(0)
    send_p(1, p1)
    pass_on_f(1)
    collect_f(1)
    collect_p(1)
    col_ref[...] = scatter_pass(1, f1, window)
    gen_ref[...] = finish_g(1)[:branches]

    def drain(j, c):
        for i in range(2):
            f_copy(i, j).wait_send()
            f_forward(i, j).wait_send()
            p_copy(i, j).wait_send()
            g_copy(i, j).wait_send()
        return c

    lax.fori_loop(1, n, drain, 0)
    for i in range(2):
        c_copy(i).wait_send()


def solution(mesh):
    n, nbr = mesh.shape["ka"], mesh.shape["br"]

    def on_device(occupation, phonons, coupling, shifted_point_index, wavevector_index, window):
        slots, branches, bands, _, width = coupling.shape
        q_width = phonons.shape[1]
        piece = width // nbr
        rows = 8
        coupling = coupling.reshape(slots, branches * bands * bands, width)
        vmem = pl.BlockSpec(memory_space=pltpu.VMEM)
        return pl.pallas_call(
            functools.partial(step_kernel, n, nbr, branches),
            out_shape=(
                jax.ShapeDtypeStruct((bands, width), F32),
                jax.ShapeDtypeStruct((branches, q_width), F32),
            ),
            in_specs=[vmem, vmem, pl.BlockSpec(memory_space=pl.ANY), vmem, vmem, vmem],
            out_specs=(vmem, vmem),
            scratch_shapes=[
                pltpu.VMEM(coupling.shape, BF16),
                pltpu.VMEM((slots, piece, width), BF16),
                pltpu.VMEM((slots, q_width, width), BF16),
                pltpu.VMEM((2, n, nbr, rows, piece), F32),
                pltpu.VMEM((2, n, rows, q_width), F32),
                pltpu.VMEM((2, n, rows, q_width), F32),
                pltpu.VMEM((2, n, rows, q_width), F32),
                pltpu.VMEM((2, bands, width), F32),
                pltpu.VMEM((2, bands, width), F32),
                pltpu.VMEM((2, n * nbr * rows, piece), BF16),
                pltpu.VMEM((2, n * rows, q_width), BF16),
                pltpu.VMEM((bands, rows, width), F32),
                pltpu.VMEM((2 * n * rows, q_width), F32),
                pltpu.VMEM((bands, rows, width), F32),
                pltpu.VMEM((bands, rows, width), F32),
                pltpu.SemaphoreType.DMA((slots,)),
            ] + [pltpu.SemaphoreType.DMA((2, n))] * 8 + [pltpu.SemaphoreType.DMA((2,))] * 2,
            compiler_params=pltpu.CompilerParams(
                collective_id=0, has_side_effects=True, vmem_limit_bytes=48 * 1024 * 1024),
            cost_estimate=pl.CostEstimate(
                flops=40 * coupling.size, bytes_accessed=2 * coupling.size, transcendentals=0),
        )(occupation, phonons, coupling, shifted_point_index, wavevector_index, window)

    return jax.shard_map(
        on_device,
        mesh=mesh,
        in_specs=(
            P(None, "ka"), P("br", "ka"), P(None, "br", None, None, "ka"),
            P(None, "ka"), P(None, "ka"), P(None, "ka"),
        ),
        out_specs=(P(None, "ka"), P("br", "ka")),
        check_vma=False,
    )
```

time: 863 us -> 71.3 us (0.08)
  blocking collectives: 310 us -> 0 us
  other arithmetic: 298 us -> 0 us
  local copies, waits for them, and re-layouts: 165 us -> 4.84 us
  waiting for transfers between devices: 68.1 us -> 0 us
  Pallas kernels: 0 us -> 65.4 us
  between operations: 14.2 us -> 0.65 us
    all_gather x4 -> x0, blocking collectives: 302 us -> none  [the longest x2 195 us: fetch_states(): lax.all_gather(occupation, 'ka', axis=1, tiled=True)]
    gather x68 -> x0, local copies, waits for them, and re-layouts: 153 us -> none  [the longest x64 87.3 us: slot_step(): phonon_at = phonon_full[:, q_rows]]
    add x98 -> x0, other arithmetic: 100 us -> none  [the longest x32 99.3 us: slot_step(): emission_sum + collected_values]
    scatter-add x32 -> x0, other arithmetic: 88.3 us -> none  [slot_step(): jax.ops.segment_sum(per_point.T, q_rows, num_segments=num_q)]
    reduce_scatter x2 -> x0, waiting for transfers between devices: 68.1 us -> none  [share_generation(): return lax.psum_scatter(term, 'ka', scatter_dimension=1, tiled=True)]
    pallas_call x0 -> x1, Pallas kernels: none -> 65.4 us  [on_device(): pl.pallas_call(functools.partial(step_kernel, n, nbr, branches), out_shap...]
    reduce_sum x64 -> x0, other arithmetic: 42.7 us -> none  [the longest x32 40.7 us: slot_step(): totals = jnp.sum(tile, axis=2)]
    dot_general x32 -> x0, other arithmetic: 40 us -> none  [slot_step(): weighted = jnp.einsum('umnk,nk->umk', tile, beyond)]
  transfers between devices with their start and end apart: 2 -> 0, of which waited for: 1 -> 0; matrix products, arithmetic and copies ran while one was open for 4% -> 0% of each run, Pallas kernels for 0% -> 0%
where the time goes in v1:
time: 71.3 us; the launch traced here: 70.9 us
  Pallas kernels  65.4 us (92%)
  local copies, waits for them, and re-layouts  4.84 us (7%)
    pallas_call x1, Pallas kernels, on_device(): pl.pallas_call(functools.partial(step_kernel, n, nbr, branches), out_shap...  65.4 us
    unnamed x12, local copies, waits for them, and re-layouts  4.84 us

profile of v1, /device:TPU:0, one launch (start us, length us, event | category | flops | bytes accessed | tf_op | source)
XLA Modules:
  0.0 70.9 jit_solution(8526277234604520877)
XLA Ops:
  0.6 0.0 copy-start
  0.6 0.7 %copy-done = s32[16,512]{1,0:T(8,128)S(1)} copy-done((s32[16,512]{1,0:T(8,128)S(1)}, s32[16,512]{1,0:T(8,128)}, u32[]{:S(2)}) %copy-start) | copy-done | bytes 32792
  1.4 0.0 copy-start.1
  1.4 0.8 %copy-done.1 = s32[16,512]{1,0:T(8,128)S(1)} copy-done((s32[16,512]{1,0:T(8,128)S(1)}, s32[16,512]{1,0:T(8,128)}, u32[]{:S(2)}) %copy-start.1) | copy-done | bytes 32792
  2.1 0.0 copy-start.2
  2.2 0.7 %copy-done.2 = f32[8,512]{1,0:T(8,128)S(1)} copy-done((f32[8,512]{1,0:T(8,128)S(1)}, f32[8,512]{1,0:T(8,128)}, u32[]{:S(2)}) %copy-start.2) | copy-done | bytes 16408
  2.9 0.0 copy-start.3
  2.9 0.7 %copy-done.3 = s32[8,512]{1,0:T(8,128)S(1)} copy-done((s32[8,512]{1,0:T(8,128)S(1)}, s32[8,512]{1,0:T(8,128)}, u32[]{:S(2)}) %copy-start.3) | copy-done | bytes 16408
  3.6 0.0 copy-start.4
  3.6 0.7 copy-done.4
  4.3 65.4 %shard_map.77 = (f32[8,512]{1,0:T(8,128)S(1)}, f32[6,256]{1,0:T(8,128)S(1)}) custom-call(f32[8,512]{1,0:T(8,128)S(1)} %copy-done.2, f32[6,256]{1,0:T(8,128)S(1)} %copy-done.4, bf16[16,384,512]{2,1,0:T(8,128)(2,1)} %bitcast.1, s32[16,512]{1,0:T(8,128)S(1)} %copy-done, s32[16,512]{1,0:T(8,128)S(1)} %copy-done.1, s32[8,512]{1,0:T(8,128)S(1)} %copy-done.3), custom_call_target="tpu_custom_call" | custom-call | flops 125829120 | bytes 6291456 | tf_op jit(solution)/shard_map/pallas_call | solution.py:278
  69.7 0.6 copy.10
  70.3 0.6 copy.11
Async XLA Ops:
  0.6 0.8 %copy-start = (s32[16,512]{1,0:T(8,128)S(1)}, s32[16,512]{1,0:T(8,128)}, u32[]{:S(2)}) copy-start(s32[16,512]{1,0:T(8,128)} %kidx_ref.1) | copy-start | bytes 98308
  1.4 0.8 %copy-start.1 = (s32[16,512]{1,0:T(8,128)S(1)}, s32[16,512]{1,0:T(8,128)}, u32[]{:S(2)}) copy-start(s32[16,512]{1,0:T(8,128)} %qidx_ref.1) | copy-start | bytes 98308
  2.1 0.7 %copy-start.2 = (f32[8,512]{1,0:T(8,128)S(1)}, f32[8,512]{1,0:T(8,128)}, u32[]{:S(2)}) copy-start(f32[8,512]{1,0:T(8,128)} %occ_ref.1) | copy-start | bytes 49156
  2.9 0.7 %copy-start.3 = (s32[8,512]{1,0:T(8,128)S(1)}, s32[8,512]{1,0:T(8,128)}, u32[]{:S(2)}) copy-start(s32[8,512]{1,0:T(8,128)} %win_ref.1) | copy-start | bytes 49156
  3.6 0.7 copy-start.4

commit v2 on v1

v2 whole, which is shorter than its diff:
```python
import functools

import jax
import jax.numpy as jnp
from jax import lax
from jax.experimental import pallas as pl
from jax.experimental.pallas import tpu as pltpu
from jax.sharding import PartitionSpec as P

MESH = pl.DeviceIdType.MESH
F32 = jnp.float32
BF16 = jnp.bfloat16
LANES = 128


def quotient(x, size):
    if size & (size - 1) == 0:
        return lax.shift_right_logical(x, jnp.int32(size.bit_length() - 1))
    return lax.div(x, jnp.int32(size))


def remainder(x, size):
    if size & (size - 1) == 0:
        return lax.bitwise_and(x, jnp.int32(size - 1))
    return lax.rem(x, jnp.int32(size))


def split_terms(x):
    high = x.astype(BF16).astype(F32)
    return high, x - high


def step_kernel(
    n, nbr, branches,
    occ_hbm, pho_hbm, coup_hbm, kidx_hbm, qidx_hbm, win_hbm,
    col_ref, gen_ref,
    occ, pho, kidx, qidx, win,
    coup, onehot_k, onehot_q, f_all, p_all, g_send, g_recv, c_send, c_recv,
    f_terms, p_terms, c_acc, g_acc, wf, ww,
    in_sem, load_sem, fs_sem, fr_sem, ws_sem, wr_sem, ps_sem, pr_sem, gs_sem, gr_sem, cs_sem, cr_sem,
):
    me = lax.axis_index("ka")
    core = lax.axis_index("br")
    slots, bands, width = coup.shape[0], occ.shape[0], occ.shape[1]
    piece = width // nbr
    q_width = pho.shape[1]
    rows = 8

    inputs = [
        pltpu.make_async_copy(src, dst, in_sem.at[a])
        for a, (src, dst) in enumerate(
            ((occ_hbm, occ), (pho_hbm, pho), (qidx_hbm, qidx), (kidx_hbm, kidx), (win_hbm, win)))]
    for copy in inputs:
        copy.start()

    def load(s):
        return pltpu.make_async_copy(coup_hbm.at[s], coup.at[s], load_sem.at[s])

    def start_load(s, c):
        load(s).start()
        return c

    def ahead(j):
        return lax.rem(me + j, n)

    def behind(j):
        return lax.rem(me - j + n, n)

    sibling = {"br": 1 - core}

    barrier = pltpu.get_barrier_semaphore()

    def greet(j, c):
        pl.semaphore_signal(barrier, inc=1, device_id={"ka": ahead(j)}, device_id_type=MESH)
        return c

    lax.fori_loop(1, n, greet, 0)
    pl.semaphore_signal(barrier, inc=1, device_id=sibling, device_id_type=MESH)
    lax.fori_loop(0, slots, start_load, 0)
    for copy in inputs:
        copy.wait()
    pl.semaphore_wait(barrier, n)

    def f_copy(i, j):
        block = f_all.at[i, me, core]
        return pltpu.make_async_remote_copy(
            block, block, fs_sem.at[i, j], fr_sem.at[i, j], device_id={"ka": ahead(j)}, device_id_type=MESH)

    def f_forward(i, j):
        block = f_all.at[i, behind(j), core]
        return pltpu.make_async_remote_copy(
            block, block, ws_sem.at[i, j], wr_sem.at[i, j], device_id=sibling, device_id_type=MESH)

    def p_copy(i, j):
        block = p_all.at[i, me]
        return pltpu.make_async_remote_copy(
            block, block, ps_sem.at[i, j], pr_sem.at[i, j], device_id={"ka": ahead(j)}, device_id_type=MESH)

    def g_copy(i, j):
        return pltpu.make_async_remote_copy(
            g_send.at[i, ahead(j)], g_recv.at[i, me], gs_sem.at[i, j], gr_sem.at[i, j],
            device_id={"ka": ahead(j)}, device_id_type=MESH)

    def c_copy(i):
        return pltpu.make_async_remote_copy(
            c_send.at[i], c_recv.at[i], cs_sem.at[i], cr_sem.at[i], device_id=sibling, device_id_type=MESH)

    def each(do):
        def body(j, c):
            do(j)
            return c
        lax.fori_loop(1, n, body, 0)

    def send_f(i, f):
        for h in range(nbr):
            f_all[i, me, h] = f[:, h * piece:(h + 1) * piece]
        each(lambda j: f_copy(i, j).start())

    def send_p(i, p):
        p_all[i, me] = p
        each(lambda j: p_copy(i, j).start())

    def pass_on_f(i):
        def forward(j):
            f_copy(i, j).wait_recv()
            f_forward(i, j).start()
        each(forward)

    def collect_f(i):
        each(lambda j: f_forward(i, j).wait_recv())

        def body(a, c):
            both = jnp.concatenate([f_all[i, a, h] for h in range(nbr)], axis=0)
            high, low = split_terms(both)
            at = pl.ds(pl.multiple_of(a * nbr * rows, nbr * rows), nbr * rows)
            f_terms[at] = high.astype(BF16)
            at = pl.ds(pl.multiple_of((n + a) * nbr * rows, nbr * rows), nbr * rows)
            f_terms[at] = low.astype(BF16)
            return c
        lax.fori_loop(0, n, body, 0)

    def collect_p(i):
        each(lambda j: p_copy(i, j).wait_recv())

        def body(a, c):
            both = jnp.concatenate([p_all[i, 2 * a], p_all[i, 2 * a + 1]], axis=0)
            high, low = split_terms(both)
            at = pl.ds(pl.multiple_of(a * 2 * rows, 2 * rows), 2 * rows)
            p_terms[at] = high.astype(BF16)
            at = pl.ds(pl.multiple_of((n + 2 * a) * rows, 2 * rows), 2 * rows)
            p_terms[at] = low.astype(BF16)
            return c
        lax.fori_loop(0, n // 2, body, 0)

    def scatter_pass(i, f, window):
        for m in range(bands):
            ww[m] = jnp.broadcast_to(window[m:m + 1], (rows, width))
            wf[m] = jnp.broadcast_to((window * f)[m:m + 1], (rows, width))
        c_acc[...] = jnp.zeros_like(c_acc)
        g_acc[...] = jnp.zeros_like(g_acc)

        def select(picked, at, count):
            half = count * rows
            index = jnp.broadcast_to(at, (rows, width))
            out = picked[:rows] + picked[half:half + rows]
            for h in range(1, count):
                first = h * rows
                here = picked[first:first + rows] + picked[half + first:half + first + rows]
                out = jnp.where(index == h, here, out)
            return out

        def gather(s):
            picked = jnp.dot(f_terms[...], onehot_k[s], preferred_element_type=F32)
            e = select(picked, quotient(kidx[pl.ds(s, 1), :], piece), n * nbr)
            picked = jnp.dot(p_terms[...], onehot_q[s], preferred_element_type=F32)
            w = select(picked, quotient(qidx[pl.ds(s, 1), :], q_width), n)
            return e, w

        def terms(s, e, w):
            sums = []
            row = lax.broadcasted_iota(jnp.int32, (rows, LANES), 0)
            for k0 in range(0, width, LANES):
                here = slice(k0, k0 + LANES)
                e1 = e[:, here]
                w1 = w[:, here]
                acc = [c_acc[m, :, here] for m in range(bands)]
                t = jnp.zeros((rows, LANES), F32)
                for u in range(branches):
                    wu = jnp.broadcast_to(w1[u:u + 1], (rows, LANES))
                    x = e1 * (wu + 1.0)
                    y = e1 + wu
                    total = None
                    for m in range(0, bands, 2):
                        first = (u * bands + m) * rows
                        g2 = coup[s, first:first + 2 * rows, here].astype(F32)
                        for d in range(2):
                            term = g2[d * rows:(d + 1) * rows] * (
                                ww[m + d, :, here] * x - wf[m + d, :, here] * y)
                            acc[m + d] = acc[m + d] + term
                            total = term if total is None else total + term
                    t = jnp.where(row == u, jnp.sum(total, axis=0, keepdims=True), t)
                for m in range(bands):
                    c_acc[m, :, here] = acc[m]
                sums.append(t)
            return jnp.concatenate(sums, axis=1)

        def scatter(s, t):
            index = jnp.broadcast_to(quotient(qidx[pl.ds(s, 1), :], q_width), (rows, width))
            parts = [jnp.where(index == h, part, 0.0) for part in split_terms(t) for h in range(n)]
            spread = jnp.concatenate(parts, axis=0).astype(BF16)
            g_acc[...] += lax.dot_general(
                spread, onehot_q[s], (((1,), (1,)), ((), ())), preferred_element_type=F32)

        def body(s, carry):
            e, w, t = carry
            if i == 0:
                load(s).wait()
            after = gather(jnp.minimum(s + 1, slots - 1))
            fresh = terms(s, e, w)
            scatter(jnp.maximum(s - 1, 0), t)
            return after + (fresh,)

        first = gather(0) + (jnp.zeros((rows, width), F32),)
        _, _, t = lax.fori_loop(0, slots, body, first)
        scatter(slots - 1, t)

        total = (g_acc[:n * rows] + g_acc[n * rows:]) * (1.0 / 16.0)
        g_send[i] = total.reshape(n, rows, q_width)
        each(lambda j: g_copy(i, j).start())
        mine = jnp.concatenate(
            [jnp.sum(c_acc[m], axis=0, keepdims=True) for m in range(bands)], axis=0)
        c_send[i] = mine
        c_copy(i).start()
        c_copy(i).wait_recv()
        return mine + c_recv[i]

    def finish_g(i):
        each(lambda j: g_copy(i, j).wait_recv())
        g_recv[i, me] = g_send[i, me]
        return jnp.sum(g_recv[i], axis=0)

    f0 = occ[...]
    window = win[...].astype(F32)
    send_f(0, f0)
    p0 = jnp.concatenate([pho[...], jnp.zeros((rows - branches, q_width), F32)], axis=0)
    send_p(0, p0)

    def build_q(s, c):
        low = remainder(qidx[pl.ds(s, 1), :], q_width)
        onehot_q[s] = jnp.where(
            lax.broadcasted_iota(jnp.int32, (q_width, width), 0) == low, 1.0, 0.0).astype(BF16)
        return c

    def build_k(s, c):
        low = remainder(kidx[pl.ds(s, 1), :], piece)
        onehot_k[s] = jnp.where(
            lax.broadcasted_iota(jnp.int32, (piece, width), 0) == low, 1.0, 0.0).astype(BF16)
        return c

    lax.fori_loop(0, slots, build_q, 0)
    pass_on_f(0)
    lax.fori_loop(0, slots, build_k, 0)
    collect_f(0)
    collect_p(0)
    c0 = scatter_pass(0, f0, window)
    f1 = f0 + 0.1 * c0
    send_f(1, f1)
    p1 = p0 + 0.1 * finish_g(0)
    send_p(1, p1)
    pass_on_f(1)
    collect_f(1)
    collect_p(1)
    col_ref[...] = scatter_pass(1, f1, window)
    gen_ref[...] = finish_g(1)[:branches]

    def drain(j, c):
        for i in range(2):
            f_copy(i, j).wait_send()
            f_forward(i, j).wait_send()
            p_copy(i, j).wait_send()
            g_copy(i, j).wait_send()
        return c

    lax.fori_loop(1, n, drain, 0)
    for i in range(2):
        c_copy(i).wait_send()


def solution(mesh):
    n, nbr = mesh.shape["ka"], mesh.shape["br"]

    def on_device(occupation, phonons, coupling, shifted_point_index, wavevector_index, window):
        slots, branches, bands, _, width = coupling.shape
        q_width = phonons.shape[1]
        piece = width // nbr
        rows = 8
        coupling = coupling.reshape(slots, branches * bands * bands, width)
        vmem = pl.BlockSpec(memory_space=pltpu.VMEM)
        return pl.pallas_call(
            functools.partial(step_kernel, n, nbr, branches),
            out_shape=(
                jax.ShapeDtypeStruct((bands, width), F32),
                jax.ShapeDtypeStruct((branches, q_width), F32),
            ),
            in_specs=[pl.BlockSpec(memory_space=pl.ANY)] * 6,
            out_specs=(vmem, vmem),
            scratch_shapes=[
                pltpu.VMEM(occupation.shape, F32),
                pltpu.VMEM(phonons.shape, F32),
                pltpu.VMEM(shifted_point_index.shape, jnp.int32),
                pltpu.VMEM(wavevector_index.shape, jnp.int32),
                pltpu.VMEM(window.shape, jnp.int32),
                pltpu.VMEM(coupling.shape, BF16),
                pltpu.VMEM((slots, piece, width), BF16),
                pltpu.VMEM((slots, q_width, width), BF16),
                pltpu.VMEM((2, n, nbr, rows, piece), F32),
                pltpu.VMEM((2, n, rows, q_width), F32),
                pltpu.VMEM((2, n, rows, q_width), F32),
                pltpu.VMEM((2, n, rows, q_width), F32),
                pltpu.VMEM((2, bands, width), F32),
                pltpu.VMEM((2, bands, width), F32),
                pltpu.VMEM((2 * n * nbr * rows, piece), BF16),
                pltpu.VMEM((2 * n * rows, q_width), BF16),
                pltpu.VMEM((bands, rows, width), F32),
                pltpu.VMEM((2 * n * rows, q_width), F32),
                pltpu.VMEM((bands, rows, width), F32),
                pltpu.VMEM((bands, rows, width), F32),
                pltpu.SemaphoreType.DMA((5,)),
                pltpu.SemaphoreType.DMA((slots,)),
            ] + [pltpu.SemaphoreType.DMA((2, n))] * 8 + [pltpu.SemaphoreType.DMA((2,))] * 2,
            compiler_params=pltpu.CompilerParams(
                collective_id=0, has_side_effects=True, vmem_limit_bytes=63 * 1024 * 1024),
            cost_estimate=pl.CostEstimate(
                flops=40 * coupling.size, bytes_accessed=2 * coupling.size, transcendentals=0),
        )(occupation, phonons, coupling, shifted_point_index, wavevector_index, window)

    return jax.shard_map(
        on_device,
        mesh=mesh,
        in_specs=(
            P(None, "ka"), P("br", "ka"), P(None, "br", None, None, "ka"),
            P(None, "ka"), P(None, "ka"), P(None, "ka"),
        ),
        out_specs=(P(None, "ka"), P("br", "ka")),
        check_vma=False,
    )
```

time: 71.3 us -> 55.9 us (0.78)
  Pallas kernels: 65.4 us -> 52.2 us
  local copies, waits for them, and re-layouts: 4.84 us -> 2.62 us
    pallas_call x1, Pallas kernels: 65.4 us -> 52.2 us  [on_device(): pl.pallas_call(functools.partial(step_kernel, n, nbr, branches), out_shap...]
    unnamed x12 -> x2, local copies, waits for them, and re-layouts: 4.84 us -> 2.62 us
where the time goes in v2:
time: 55.9 us; the launch traced here: 55.4 us
  Pallas kernels  52.2 us (93%)
  local copies, waits for them, and re-layouts  2.62 us (5%)
  between operations  0.64 us (1%)
    pallas_call x1, Pallas kernels, on_device(): pl.pallas_call(functools.partial(step_kernel, n, nbr, branches), out_shap...  52.2 us
    unnamed x2, local copies, waits for them, and re-layouts  2.62 us

profile of v2, /device:TPU:0, one launch (start us, length us, event | category | flops | bytes accessed | tf_op | source)
XLA Modules:
  0.0 55.4 jit_solution(2931033662205610070)
XLA Ops:
  0.6 52.2 %shard_map.77 = (f32[8,512]{1,0:T(8,128)}, f32[6,256]{1,0:T(8,128)}) custom-call(f32[8,512]{1,0:T(8,128)} %occ_hbm.1, f32[6,256]{1,0:T(8,128)} %pho_hbm.1, bf16[16,384,512]{2,1,0:T(8,128)(2,1)} %bitcast.1, s32[16,512]{1,0:T(8,128)} %kidx_hbm.1, s32[16,512]{1,0:T(8,128)} %qidx_hbm.1, s32[8,512]{1,0:T(8,128)} %win_hbm.1), custom_call_target="tpu_custom_call" | custom-call | flops 125829120 | bytes 6291456 | tf_op jit(solution)/shard_map/pallas_call | solution.py:299
  52.8 1.3 %copy.10 = f32[8,512]{1,0:T(8,128)} copy(f32[8,512]{1,0:T(8,128)} %get-tuple-element.4) | data formatting | bytes 32768
  54.1 1.3 %copy.11 = f32[6,256]{1,0:T(8,128)} copy(f32[6,256]{1,0:T(8,128)} %get-tuple-element.5) | data formatting | bytes 12288

commit v3 on v2

--- a/solution.py
+++ b/solution.py
@@ -35,8 +35,8 @@
     occ_hbm, pho_hbm, coup_hbm, kidx_hbm, qidx_hbm, win_hbm,
     col_ref, gen_ref,
     occ, pho, kidx, qidx, win,
-    coup, onehot_k, onehot_q, f_all, p_all, g_send, g_recv, c_send, c_recv,
-    f_terms, p_terms, c_acc, g_acc, wf, ww,
+    coup, onehot_q, f_all, p_all, g_send, g_recv, c_send, c_recv,
+    p_terms, c_acc, g_acc, wf, ww,
     in_sem, load_sem, fs_sem, fr_sem, ws_sem, wr_sem, ps_sem, pr_sem, gs_sem, gr_sem, cs_sem, cr_sem,
 ):
     me = lax.axis_index("ka")
@@ -128,16 +128,6 @@
 
     def collect_f(i):
         each(lambda j: f_forward(i, j).wait_recv())
-
-        def body(a, c):
-            both = jnp.concatenate([f_all[i, a, h] for h in range(nbr)], axis=0)
-            high, low = split_terms(both)
-            at = pl.ds(pl.multiple_of(a * nbr * rows, nbr * rows), nbr * rows)
-            f_terms[at] = high.astype(BF16)
-            at = pl.ds(pl.multiple_of((n + a) * nbr * rows, nbr * rows), nbr * rows)
-            f_terms[at] = low.astype(BF16)
-            return c
-        lax.fori_loop(0, n, body, 0)
 
     def collect_p(i):
         each(lambda j: p_copy(i, j).wait_recv())
@@ -170,8 +160,20 @@
             return out
 
         def gather(s):
-            picked = jnp.dot(f_terms[...], onehot_k[s], preferred_element_type=F32)
-            e = select(picked, quotient(kidx[pl.ds(s, 1), :], piece), n * nbr)
+            k_index = kidx[pl.ds(s, 1), :]
+            columns = []
+            for k0 in range(0, width, LANES):
+                at = jnp.broadcast_to(k_index[:, k0:k0 + LANES], (rows, LANES))
+                lane, group = remainder(at, LANES), quotient(at, LANES)
+                e = jnp.zeros((rows, LANES), F32)
+                for h in range(n * width // LANES):
+                    owner, rest = divmod(h * LANES, width)
+                    half, first = divmod(rest, piece)
+                    block = f_all[i, owner, half, :, first:first + LANES]
+                    found = jnp.take_along_axis(block, lane, axis=1, mode="promise_in_bounds")
+                    e = jnp.where(group == h, found, e)
+                columns.append(e)
+            e = jnp.concatenate(columns, axis=1)
             picked = jnp.dot(p_terms[...], onehot_q[s], preferred_element_type=F32)
             w = select(picked, quotient(qidx[pl.ds(s, 1), :], q_width), n)
             return e, w
@@ -251,15 +253,8 @@
             lax.broadcasted_iota(jnp.int32, (q_width, width), 0) == low, 1.0, 0.0).astype(BF16)
         return c
 
-    def build_k(s, c):
-        low = remainder(kidx[pl.ds(s, 1), :], piece)
-        onehot_k[s] = jnp.where(
-            lax.broadcasted_iota(jnp.int32, (piece, width), 0) == low, 1.0, 0.0).astype(BF16)
-        return c
-
     lax.fori_loop(0, slots, build_q, 0)
     pass_on_f(0)
-    lax.fori_loop(0, slots, build_k, 0)
     collect_f(0)
     collect_p(0)
     c0 = scatter_pass(0, f0, window)
@@ -311,7 +306,6 @@
                 pltpu.VMEM(wavevector_index.shape, jnp.int32),
                 pltpu.VMEM(window.shape, jnp.int32),
                 pltpu.VMEM(coupling.shape, BF16),
-                pltpu.VMEM((slots, piece, width), BF16),
                 pltpu.VMEM((slots, q_width, width), BF16),
                 pltpu.VMEM((2, n, nbr, rows, piece), F32),
                 pltpu.VMEM((2, n, rows, q_width), F32),
@@ -319,7 +313,6 @@
                 pltpu.VMEM((2, n, rows, q_width), F32),
                 pltpu.VMEM((2, bands, width), F32),
                 pltpu.VMEM((2, bands, width), F32),
-                pltpu.VMEM((2 * n * nbr * rows, piece), BF16),
                 pltpu.VMEM((2 * n * rows, q_width), BF16),
                 pltpu.VMEM((bands, rows, width), F32),
                 pltpu.VMEM((2 * n * rows, q_width), F32),

time: 55.9 us -> 56.8 us (1.016)
  Pallas kernels: 52.2 us -> 53.2 us
    pallas_call x1, Pallas kernels: 52.2 us -> 53.2 us  [on_device(): pl.pallas_call(functools.partial(step_kernel, n, nbr, branches), out_shap...]
where the time goes in v3:
time: 56.8 us; the launch traced here: 56.4 us
  Pallas kernels  53.2 us (94%)
  local copies, waits for them, and re-layouts  2.62 us (5%)
  between operations  0.64 us (1%)
    pallas_call x1, Pallas kernels, on_device(): pl.pallas_call(functools.partial(step_kernel, n, nbr, branches), out_shap...  53.2 us
    unnamed x2, local copies, waits for them, and re-layouts  2.62 us

profile of v3, /device:TPU:0, one launch (start us, length us, event | category | flops | bytes accessed | tf_op | source)
XLA Modules:
  0.0 56.4 jit_solution(2990220247771462855)
XLA Ops:
  0.6 53.2 %shard_map.77 = (f32[8,512]{1,0:T(8,128)}, f32[6,256]{1,0:T(8,128)}) custom-call(f32[8,512]{1,0:T(8,128)} %occ_hbm.1, f32[6,256]{1,0:T(8,128)} %pho_hbm.1, bf16[16,384,512]{2,1,0:T(8,128)(2,1)} %bitcast.1, s32[16,512]{1,0:T(8,128)} %kidx_hbm.1, s32[16,512]{1,0:T(8,128)} %qidx_hbm.1, s32[8,512]{1,0:T(8,128)} %win_hbm.1), custom_call_target="tpu_custom_call" | custom-call | flops 125829120 | bytes 6291456 | tf_op jit(solution)/shard_map/pallas_call | solution.py:294
  53.8 1.3 %copy.10 = f32[8,512]{1,0:T(8,128)} copy(f32[8,512]{1,0:T(8,128)} %get-tuple-element.4) | data formatting | bytes 32768
  55.1 1.3 %copy.11 = f32[6,256]{1,0:T(8,128)} copy(f32[6,256]{1,0:T(8,128)} %get-tuple-element.5) | data formatting | bytes 12288
